TPU v7x, 32 devices: a whole 2x2x4 slice. The times are simulated.
32 devices in a mesh: dp: 16 (over z, y, core), tensor: 2 (over x).
Axes of the slice: x: 2, y: 2, z: 4, core: 2. Of those that a mesh axis runs over, the one named last changes fastest.
Arguments:
- acts: bfloat16 [16384, 8192], P('dp', 'tensor'), may hold values from -6 to 6
- out_grads: bfloat16 [16384, 28672], P('dp', 'tensor'), may hold values from -6 to 6
- proj_in: bfloat16 [64, 8192], P(None, 'tensor'), may hold values from -0.0625 to 0.0625
- proj_out: bfloat16 [64, 28672], P(None, 'tensor'), may hold values from -0.03125 to 0.03125
- lengths: int32 [64], P('dp'), may hold values from 1 to 256, 8192 in all
- queries: float32 [512, 4096], P('tensor', 'dp'), may hold values from -6 to 6
- query_ids: int32 [512], P('tensor'), may hold values from 0 to 63
Outputs:
- scores: float32 [64, 512], P('dp', 'tensor')
All inputs are finite; a program needn't handle non-finite values. No bound on the sum of `lengths` on one device may be relied on, other than what follows from the above.
Results may differ from a plain program's by a relative error of at most 0.0003.
Values sent between devices are 32-bit elements; how exact they have to be, the bound alone decides.
No kernel may reach another device: no remote copies, remote signals or barrier semaphores. Data moves between devices by JAX's collectives and lax.ppermute only.
A program may use at most 128 MiB of HBM per device.

v0:
```python
import jax
import jax.numpy as jnp
from jax import lax
from jax.sharding import PartitionSpec as P


def contract_rows(left, right):
    return lax.dot_general(
        left, right, (((1,), (1,)), ((), ())), preferred_element_type=jnp.float32
    )


def contract_exact(left, right):
    return lax.dot_general(
        left,
        right,
        (((1,), (1,)), ((), ())),
        precision=lax.Precision.HIGHEST,
        preferred_element_type=jnp.float32,
    )


def slot_kron(summed, lengths, rank_out):
    slot_count = summed.shape[1]
    grads_ex = summed[:, :, :rank_out]
    acts_ex = summed[:, :, rank_out:]
    position = lax.broadcasted_iota(jnp.int32, (summed.shape[0], slot_count), 1)
    valid = (position < lengths[:, None]).astype(jnp.float32)
    kron = jnp.einsum(
        "eso,esi->eoi", grads_ex * valid[:, :, None], acts_ex, precision=lax.Precision.HIGHEST
    )
    return kron.reshape(summed.shape[0], -1)


def on_device(acts, out_grads, proj_in, proj_out, lengths, queries, query_ids):
    rank_out = proj_out.shape[0]
    ex_count = lengths.shape[0]
    slot_len = acts.shape[0] // ex_count
    part_grads = contract_rows(out_grads, proj_out)
    part_acts = contract_rows(acts, proj_in)
    joined = jnp.concatenate([part_grads, part_acts], axis=1)
    summed = lax.psum(joined, "tensor")
    kron = slot_kron(summed.reshape(ex_count, slot_len, -1), lengths, rank_out)
    unit = kron / jnp.sqrt(jnp.sum(kron * kron, axis=1, keepdims=True) + 1e-06)
    scores = contract_exact(unit, lax.all_gather(queries, "dp", axis=1, tiled=True))
    example_ids = lax.axis_index("dp") * ex_count + lax.broadcasted_iota(
        jnp.int32, (ex_count, 1), 0
    )
    same = example_ids == query_ids[None, :]
    return jnp.where(same, jnp.zeros_like(scores), scores)


def solution(mesh):
    in_specs = (
        P("dp", "tensor"),
        P("dp", "tensor"),
        P(None, "tensor"),
        P(None, "tensor"),
        P("dp"),
        P("tensor", "dp"),
        P("tensor"),
    )
    out_specs = P("dp", "tensor")
    return jax.shard_map(
        on_device, mesh=mesh, in_specs=in_specs, out_specs=out_specs, check_vma=False
    )
```

profile of v0, /device:TPU:0, one launch (start us, length us, event | category | flops | bytes accessed | tf_op | source)
XLA Modules:
  0.0 101.9 jit_solution(7786130688410789780)
XLA Ops:
  7.4 0.0 copy-start
  7.4 0.0 copy-start.1
  7.4 0.0 all-reduce.2.cloned.1.call-start
  7.4 1.5 %copy-done = bf16[64,14336]{1,0:T(8,128)(2,1)S(1)} copy-done((bf16[64,14336]{1,0:T(8,128)(2,1)S(1)}, bf16[64,14336]{1,0:T(8,128)(2,1)}, u32[]{:S(2)}) %copy-start) | copy-done | bytes 1835032
  8.9 14.3 %fusion.6 = f32[1024,64]{0,1:T(8,128)S(1)} fusion(bf16[1024,14336]{1,0:T(8,128)(2,1)} %param.8, bf16[64,14336]{1,0:T(8,128)(2,1)S(1)} %copy-done), kind=kOutput, calls=%fused_computation.14 | convolution fusion | flops 1879048192 | bytes 31457280 | tf_op jit(solution)/shard_map/dot_general | solution.py:8
  23.2 0.0 copy-done.1
  23.2 0.0 copy-start.3
  23.2 0.0 copy-start.2
  23.2 6.0 %fusion.7 = f32[1024,64]{0,1:T(8,128)S(1)} fusion(bf16[1024,4096]{1,0:T(8,128)(2,1)} %param.7, bf16[64,4096]{1,0:T(8,128)(2,1)S(1)} %copy-done.1), kind=kOutput, calls=%fused_computation.15 | convolution fusion | flops 536870912 | bytes 9175040 | tf_op jit(solution)/shard_map/dot_general | solution.py:8
  29.3 0.8 copy.11
  30.2 0.0 all-reduce.2.cloned.1.call-update
  30.2 0.0 all-gather.2.cloned.1.call-start
  30.2 0.5 all-gather.2.cloned.1.call-update
  30.8 0.0 copy-done.3
  30.8 0.1 fusion.5
  30.9 30.8 %all-reduce.2.cloned.1.call-done = f32[4,256,128]{1,2,0:T(8,128)} async-done(((f32[4,256,128]{1,2,0:T(8,128)}), f32[4,256,128]{1,2,0:T(8,128)}) %all-reduce.2.cloned.1.call-update) | async-done | bytes 524304 | tf_op jit(solution)/shard_map/psum | solution.py:42
  61.7 1.5 %multiply_reduce_fusion = (f32[4]{0:T(128)S(1)}, f32[4,64,64]{2,1,0:T(8,128)S(1)}) fusion(f32[4,256,128]{1,2,0:T(8,128)} %all-reduce.2.cloned.1.call-done, f32[4,256]{1,0:T(4,128)S(1)} %fusion.5), kind=kOutput, calls=%fused_computation.6 | convolution fusion | flops 50429948 | bytes 593936 | tf_op jit(solution)/shard_map/eso,esi->eoi/dot_general | solution.py:29
  63.2 0.1 reshape.39
  63.3 25.0 %all-gather.2.cloned.1.call-done = f32[256,4096]{1,0:T(8,128)} async-done(((f32[256,256]{1,0:T(8,128)}), f32[256,4096]{1,0:T(8,128)}) %all-gather.2.cloned.1.call-update) | async-done | bytes 4194320 | tf_op jit(solution)/shard_map/all_gather | solution.py:45
  88.3 0.0 copy-done.2
  88.3 6.1 %convolution_select_fusion = f32[4,256]{1,0:T(4,128)} fusion(f32[256,4096]{1,0:T(8,128)} %all-gather.2.cloned.1.call-done, f32[4,4096]{1,0:T(4,128)S(1)} %reshape.39, f32[4]{0:T(128)S(1)} %add_sqrt_fusion, s32[256]{0:T(256)S(1)} %copy-done.2, s32[4]{0:T(128)S(1)} %iota_add_fusion), kind=kOutput, calls=%fused_computation | convolution fusion | flops 50350080 | bytes 4264992 | tf_op jit(solution)/shard_map/dot_general | solution.py:14
  (3 shorter events, 0.0 us)
Async XLA Ops:
  7.4 1.5 %copy-start = (bf16[64,14336]{1,0:T(8,128)(2,1)S(1)}, bf16[64,14336]{1,0:T(8,128)(2,1)}, u32[]{:S(2)}) copy-start(bf16[64,14336]{1,0:T(8,128)(2,1)} %param.10) | copy-start | bytes 5505028
  7.4 15.8 %copy-start.1 = (bf16[64,4096]{1,0:T(8,128)(2,1)S(1)}, bf16[64,4096]{1,0:T(8,128)(2,1)}, u32[]{:S(2)}) copy-start(bf16[64,4096]{1,0:T(8,128)(2,1)} %param.9) | copy-start | bytes 1572868
  7.4 54.3 %all-reduce.2.cloned.1.call-start = ((), (), s32[]{:S(2)}) async-start(), calls=%async_computation | async-start | bytes 1048576 | tf_op jit(solution)/shard_map/psum | solution.py:42
  23.2 7.6 %copy-start.3 = (s32[4]{0:T(128)S(1)}, s32[4]{0:T(128)}, u32[]{:S(2)}) copy-start(s32[4]{0:T(128)} %param.11) | copy-start | bytes 52
  23.2 65.1 %copy-start.2 = (s32[256]{0:T(256)S(1)}, s32[256]{0:T(256)}, u32[]{:S(2)}) copy-start(s32[256]{0:T(256)} %param.13) | copy-start | bytes 3076
  30.2 58.1 %all-gather.2.cloned.1.call-start = ((), (), s32[]{:S(2)}) async-start(), calls=%async_computation.1 | async-start | bytes 4456448 | tf_op jit(solution)/shard_map/all_gather | solution.py:45
Sparse Core Ops, SparseCore 0:
  30.3 31.3 all-reduce.1
Sparse Core Ops, SparseCore 1:
  32.8 55.4 all-gather.1
where the time goes:
time: 102 us
  waiting for transfers between devices  56.4 us (55%)
  matrix products  28 us (27%)
  between operations  14.9 us (15%)
  local copies, waits for them, and re-layouts  2.47 us (2%)
    psum x1, waiting for transfers between devices, on_device(): summed = lax.psum(joined, 'tensor')  30.8 us
    all_gather x1, waiting for transfers between devices, on_device(): lax.all_gather(queries, 'dp', axis=1, tiled=True)  25 us
    dot_general x2, matrix products, contract_rows(): lax.dot_general(left, right, (((1,), (1,)), ((), ())), preferred_element_...  20.3 us
    dot_general x1, matrix products, contract_exact(): lax.dot_general(left, right, (((1,), (1,)), ((), ())), precision=lax.Prec...  6.14 us
  transfers between devices with their start and end apart: 2, of which 2 were waited for; matrix products, arithmetic and copies ran while one was open for 2% of the time, Pallas kernels for 0%

commit v1 on v0

v1 whole, which is shorter than its diff:
```python
import functools

import jax
import jax.numpy as jnp
from jax import lax
from jax.experimental import pallas as pl
from jax.experimental.pallas import tpu as pltpu
from jax.sharding import PartitionSpec as P

BLOCK = 64
NEAR = 8
NT = (((1,), (1,)), ((), ()))
TN = (((0,), (0,)), ((), ()))
ANY = pl.BlockSpec(memory_space=pl.ANY)
VMEM = pl.BlockSpec(memory_space=pltpu.VMEM)


def xor_pairs(size, mask):
    return [(i, i ^ mask) for i in range(size)]


def swap(x, mask):
    return lax.ppermute(x, "dp", xor_pairs(lax.axis_size("dp"), mask))


def project_kernel(peer, count, slot, lengths, acts, grads, proj_in, proj_out, out,
                   used, act_buf, grad_buf, in_buf, out_buf, sems, small):
    per = slot // BLOCK
    blocks = count * per
    first = 0
    if peer is not None:
        mine = lax.axis_index("tensor")
        first = (1 - mine if peer else mine) * count
    rank = proj_out.shape[0]

    def copies(j):
        row = pl.multiple_of(first * slot + j * BLOCK, BLOCK)
        return (
            pltpu.make_async_copy(grads.at[pl.ds(row, BLOCK)], grad_buf.at[j], sems.at[0, j]),
            pltpu.make_async_copy(acts.at[pl.ds(row, BLOCK)], act_buf.at[j], sems.at[1, j]),
        )

    def left(j):
        return used[first + j // per] - (j % per) * BLOCK

    get_used = pltpu.make_async_copy(lengths, used, small.at[0])
    get_out = pltpu.make_async_copy(proj_out, out_buf, small.at[1])
    get_in = pltpu.make_async_copy(proj_in, in_buf, small.at[2])
    get_used.start()
    get_out.start()
    get_in.start()
    get_used.wait()

    @pl.loop(0, blocks)
    def _(j):
        @pl.when(left(j) > 0)
        def _():
            for copy in copies(j):
                copy.start()

    get_out.wait()
    get_in.wait()

    @pl.loop(0, blocks)
    def _(j):
        rows = left(j)

        @pl.when(rows > 0)
        def _():
            for copy in copies(j):
                copy.wait()
            part_grads = lax.dot_general(
                grad_buf[j], out_buf[...], NT, preferred_element_type=jnp.float32
            )
            part_acts = lax.dot_general(
                act_buf[j], in_buf[...], NT, preferred_element_type=jnp.float32
            )
            joined = jnp.concatenate([part_grads, part_acts], axis=1)
            row = lax.broadcasted_iota(jnp.int32, joined.shape, 0)
            out[j] = jnp.where(row < rows, joined, 0.0)

        @pl.when(rows <= 0)
        def _():
            out[j] = jnp.zeros((BLOCK, 2 * rank), jnp.float32)


def project(peer, count, slot, lengths, acts, grads, proj_in, proj_out):
    blocks = count * slot // BLOCK
    width = proj_out.shape[0] + proj_in.shape[0]
    rows = blocks * BLOCK
    bytes_accessed = 2 * (rows + width // 2) * (acts.shape[1] + grads.shape[1])
    return pl.pallas_call(
        functools.partial(project_kernel, peer, count, slot),
        out_shape=jax.ShapeDtypeStruct((blocks, BLOCK, width), jnp.float32),
        in_specs=[ANY] * 5,
        out_specs=VMEM,
        scratch_shapes=[
            pltpu.SMEM(lengths.shape, jnp.int32),
            pltpu.VMEM((blocks, BLOCK, acts.shape[1]), acts.dtype),
            pltpu.VMEM((blocks, BLOCK, grads.shape[1]), grads.dtype),
            pltpu.VMEM(proj_in.shape, proj_in.dtype),
            pltpu.VMEM(proj_out.shape, proj_out.dtype),
            pltpu.SemaphoreType.DMA((2, blocks)),
            pltpu.SemaphoreType.DMA((3,)),
        ],
        compiler_params=pltpu.CompilerParams(vmem_limit_bytes=44 << 20),
        cost_estimate=pl.CostEstimate(
            flops=width * rows * (acts.shape[1] + grads.shape[1]),
            bytes_accessed=bytes_accessed,
            transcendentals=0,
        ),
        name="project",
    )(lengths, acts, grads, proj_in, proj_out)


def unit_kernel(count, slot, rank, *refs):
    parts, outs, square, cols = refs[:-3], refs[-3], refs[-2], refs[-1]
    near = outs.shape[2]
    group = lax.axis_index("dp") // near
    split, per = cols.shape[1], square.shape[0] // cols.shape[1]
    for e in range(count):
        total = parts[0][e]
        for part in parts[1:]:
            total = total + part[e]
        kron = lax.dot_general(
            total[:, :rank], total[:, rank:], TN,
            precision=lax.Precision.HIGHEST, preferred_element_type=jnp.float32,
        )
        norm = jnp.sqrt(jnp.sum(kron * kron, keepdims=True) + 1e-06)
        square[...] = kron / norm
        cols[e] = jnp.concatenate(
            [square[pl.ds(c, split, stride=per), :] for c in range(per)], axis=1
        )
        for r in range(outs.shape[0]):
            start = pl.multiple_of((group ^ r) * near, near)
            outs[r, e] = cols[e, pl.ds(start, near), :]


def units(parts, count, slot, rank, split):
    width = parts[0].shape[-1]
    rest = width - rank
    near = min(NEAR, split)
    parts = [part.reshape(count, slot, width) for part in parts]
    return pl.pallas_call(
        functools.partial(unit_kernel, count, slot, rank),
        out_shape=jax.ShapeDtypeStruct(
            (split // near, count, near, rank * rest // split), jnp.float32
        ),
        in_specs=[VMEM] * len(parts),
        out_specs=VMEM,
        scratch_shapes=[
            pltpu.VMEM((rank, rest), jnp.float32),
            pltpu.VMEM((count, split, rank * rest // split), jnp.float32),
        ],
        name="units",
    )(*parts)


def hi_lo(x):
    hi = x.astype(jnp.bfloat16)
    return hi, (x - hi.astype(jnp.float32)).astype(jnp.bfloat16)


def score_kernel(sources, *refs):
    rows_of, blocks, out = refs[:sources], refs[sources:-1], refs[-1]
    low = lax.axis_index("dp") % len(blocks)
    count = rows_of[0].shape[0]
    total = jnp.zeros(out.shape, jnp.float32)
    for m, block in enumerate(blocks):
        rows = jnp.concatenate(
            [ref[e, pl.ds(low ^ m, 1), :] for ref in rows_of for e in range(count)], axis=0
        )
        rows_hi, rows_lo = hi_lo(rows)
        block_hi, block_lo = hi_lo(block[...])
        both = lax.dot_general(
            jnp.concatenate([rows_hi, rows_lo], axis=0), block_hi, NT,
            preferred_element_type=jnp.float32,
        )
        cross = lax.dot_general(rows_hi, block_lo, NT, preferred_element_type=jnp.float32)
        total = total + (both[: rows.shape[0]] + (both[rows.shape[0] :] + cross))
    out[...] = total


def partial_scores(rows_of, blocks):
    rows = sum(part.shape[0] for part in rows_of)
    return pl.pallas_call(
        functools.partial(score_kernel, len(rows_of)),
        out_shape=jax.ShapeDtypeStruct((rows, blocks[0].shape[0]), jnp.float32),
        in_specs=[VMEM] * (len(rows_of) + len(blocks)),
        out_specs=VMEM,
        name="scores",
    )(*rows_of, *blocks)


def gather_near(queries, near):
    blocks = {0: queries}
    if near == 8:
        half = queries.shape[0] // 2
        blocks[2] = swap(queries, 2)
        blocks[4] = swap(queries, 4)
        blocks[6] = jnp.concatenate(
            [swap(blocks[4][:half], 2), swap(blocks[2][half:], 4)], axis=0
        )
        for m in (0, 2, 4, 6):
            blocks[m ^ 1] = swap(blocks[m], 1)
    else:
        for m in range(1, near):
            blocks[m] = swap(queries, m)
    return [blocks[m] for m in range(near)]


def on_device(acts, out_grads, proj_in, proj_out, lengths, queries, query_ids):
    rank_out = proj_out.shape[0]
    ex_count = lengths.shape[0]
    slot = acts.shape[0] // ex_count
    split = lax.axis_size("dp")
    near = min(NEAR, split)
    tensors = lax.axis_size("tensor")
    halves = tensors == 2 and ex_count % 2 == 0
    args = (lengths, acts, out_grads, proj_in, proj_out)
    blocks = gather_near(queries, near)
    if halves:
        count = ex_count // 2
        theirs = project(True, count, slot, *args)
        arrived = lax.ppermute(theirs, "tensor", [(0, 1), (1, 0)])
        mine = project(False, count, slot, *args)
        parts = [mine, arrived]
    else:
        count = ex_count
        parts = [lax.psum(project(None, count, slot, *args), "tensor")]
    unit = units(parts, count, slot, rank_out, split)
    rows_of = []
    for r in range(split // near):
        got = unit[r]
        far = got if r == 0 else swap(got, r * near)
        rows_of.append(far)
        if halves:
            both = [(2 * i + t, 2 * (i ^ (r * near)) + 1 - t) for i in range(split) for t in (0, 1)]
            rows_of.append(lax.ppermute(got, ("dp", "tensor"), both))
    sums = partial_scores(rows_of, blocks)
    sums = sums.reshape(split // near, ex_count, -1)
    scores = sums[0]
    for r in range(1, split // near):
        scores = scores + swap(sums[r], r * near)
    if halves:
        scores = jnp.where(
            lax.axis_index("tensor") == 0, scores, jnp.roll(scores, count, axis=0)
        )
    example_ids = lax.axis_index("dp") * ex_count + lax.broadcasted_iota(
        jnp.int32, (ex_count, 1), 0
    )
    same = example_ids == query_ids[None, :]
    return jnp.where(same, jnp.zeros_like(scores), scores)


def solution(mesh):
    in_specs = (
        P("dp", "tensor"),
        P("dp", "tensor"),
        P(None, "tensor"),
        P(None, "tensor"),
        P("dp"),
        P("tensor", "dp"),
        P("tensor"),
    )
    out_specs = P("dp", "tensor")
    return jax.shard_map(
        on_device, mesh=mesh, in_specs=in_specs, out_specs=out_specs, check_vma=False
    )
```

time: 102 us -> 58.4 us (0.57)
  waiting for transfers between devices: 56.4 us -> 14.8 us
  matrix products: 28 us -> 0 us
  starting transfers between devices: 0.05 us -> 17.2 us
  Pallas kernels: 0 us -> 16.6 us
  between operations: 14.9 us -> 0.18 us
  local copies, waits for them, and re-layouts: 2.47 us -> 7.59 us
  other arithmetic: 0.12 us -> 1.37 us
    psum x1 -> x0, waiting for transfers between devices: 30.8 us -> none  [on_device(): summed = lax.psum(joined, 'tensor')]
    dot_general x4 -> x0, matrix products: 28 us -> none  [the longest x2 20.3 us: contract_rows(): lax.dot_general(left, right, (((1,), (1,)), ((), ())), preferred_element_...]
    all_gather x1 -> x0, waiting for transfers between devices: 25 us -> none  [on_device(): lax.all_gather(queries, 'dp', axis=1, tiled=True)]
    ppermute x0 -> x13, starting transfers between devices: none -> 17.2 us  [the longest x10 12.8 us: swap(): return lax.ppermute(x, 'dp', xor_pairs(lax.axis_size('dp'), mask))]
    pallas_call x0 -> x4, Pallas kernels: none -> 16.6 us  [the longest x2 11.6 us: project(): pl.pallas_call(functools.partial(project_kernel, peer, count, slot), out_...]
    ppermute x0 -> x13, waiting for transfers between devices: none -> 14.8 us  [the longest x10 10.5 us: swap(): return lax.ppermute(x, 'dp', xor_pairs(lax.axis_size('dp'), mask))]
    unnamed x8 -> x35, local copies, waits for them, and re-layouts: 1.51 us -> 6.12 us
  transfers between devices with their start and end apart: 2 -> 13, of which waited for: 2 -> 5; matrix products, arithmetic and copies ran while one was open for 2% -> 1% of each run, Pallas kernels for 0% -> 24%
where the time goes in v1:
time: 58.4 us; the launch traced here: 57.8 us
  starting transfers between devices  17.2 us (29%)
  Pallas kernels  16.6 us (28%)
  waiting for transfers between devices  14.8 us (25%)
  local copies, waits for them, and re-layouts  7.59 us (13%)
  other arithmetic  1.37 us (2%)
    ppermute x10, starting transfers between devices, swap(): return lax.ppermute(x, 'dp', xor_pairs(lax.axis_size('dp'), mask))  12.8 us
    pallas_call x2, Pallas kernels, project(): pl.pallas_call(functools.partial(project_kernel, peer, count, slot), out_...  11.6 us
    ppermute x10, waiting for transfers between devices, swap(): return lax.ppermute(x, 'dp', xor_pairs(lax.axis_size('dp'), mask))  10.5 us
    unnamed x35, local copies, waits for them, and re-layouts  6.12 us
    ppermute x2, starting transfers between devices, on_device(): rows_of.append(lax.ppermute(got, ('dp', 'tensor'), both))  4.37 us
    ppermute x2, waiting for transfers between devices, on_device(): rows_of.append(lax.ppermute(got, ('dp', 'tensor'), both))  4.31 us
    pallas_call x1, Pallas kernels, partial_scores(): pl.pallas_call(functools.partial(score_kernel, len(rows_of)), out_shape=j...  2.82 us
    pallas_call x1, Pallas kernels, units(): pl.pallas_call(functools.partial(unit_kernel, count, slot, rank), out_sha...  2.26 us
  transfers between devices with their start and end apart: 13, of which 5 were waited for; matrix products, arithmetic and copies ran while one was open for 1% of the time, Pallas kernels for 24%

profile of v1, /device:TPU:0, one launch (start us, length us, event | category | flops | bytes accessed | tf_op | source)
XLA Modules:
  0.0 57.8 jit_solution(14055911460649227712)
XLA Ops:
  0.0 3.0 %collective-permute-start.7 = (f32[256,256]{1,0:T(8,128)}, f32[256,256]{1,0:T(8,128)S(1)}, u32[]{:S(2)}, u32[]{:S(2)}) collective-permute-start(f32[256,256]{1,0:T(8,128)} %refs_4_.1), channel_id=1, source_target_pairs={{0,8},{2,10},{4,12},{6,14},{8,0},{10,2},{12,4},{14,6},{16,24},{18,... | collective-permute-start | bytes 786440 | tf_op jit(solution)/shard_map/ppermute | solution.py:23
  3.0 1.5 %collective-permute-start.5 = (f32[256,256]{1,0:T(8,128)}, f32[256,256]{1,0:T(8,128)S(1)}, u32[]{:S(2)}, u32[]{:S(2)}) collective-permute-start(f32[256,256]{1,0:T(8,128)} %refs_4_.1), channel_id=1, source_target_pairs={{0,4},{2,6},{4,0},{6,2},{8,12},{10,14},{12,8},{14,10},{16,20},{18,... | collective-permute-start | bytes 786440 | tf_op jit(solution)/shard_map/ppermute | solution.py:23
  4.5 5.0 %collective-permute-done.7.refs_8_ = f32[256,256]{1,0:T(8,128)S(1)} collective-permute-done((f32[256,256]{1,0:T(8,128)}, f32[256,256]{1,0:T(8,128)S(1)}, u32[]{:S(2)}, u32[]{:S(2)}) %collective-permute-start.7) | collective-permute-done | bytes 262176 | tf_op jit(solution)/shard_map/ppermute | solution.py:23
  9.6 1.8 %collective-permute-start.9 = (f32[128,256]{1,0:T(8,128)S(1)}, f32[128,256]{1,0:T(8,128)S(1)}, u32[]{:S(2)}, u32[]{:S(2)}) collective-permute-start(f32[128,256]{1,0:T(8,128)S(1)} %slice.38), channel_id=1, source_target_pairs={{0,4},{2,6},{4,0},{6,2},{8,12},{10,14},{12,8},{14,10},{16,20},{18,... | collective-permute-start | bytes 393224 | tf_op jit(solution)/shard_map/ppermute | solution.py:23
  11.3 0.0 collective-permute-start.4
  11.3 0.0 collective-permute-done.5.refs_6_
  11.3 1.6 %collective-permute-start.10 = (f32[128,256]{1,0:T(8,128)S(1)}, f32[128,256]{1,0:T(8,128)S(1)}, u32[]{:S(2)}, u32[]{:S(2)}) collective-permute-start(f32[128,256]{1,0:T(8,128)S(1)} %slice.39), channel_id=1, source_target_pairs={{0,8},{2,10},{4,12},{6,14},{8,0},{10,2},{12,4},{14,6},{16,24},{18,... | collective-permute-start | bytes 393224 | tf_op jit(solution)/shard_map/ppermute | solution.py:23
  13.0 1.5 %copy-done = bf16[64,14336]{1,0:T(8,128)(2,1)S(1)} copy-done((bf16[64,14336]{1,0:T(8,128)(2,1)S(1)}, bf16[64,14336]{1,0:T(8,128)(2,1)}, u32[]{:S(2)}) %copy-start) | copy-done | bytes 1835032
  14.5 1.0 %copy-done.1 = bf16[64,4096]{1,0:T(8,128)(2,1)S(1)} copy-done((bf16[64,4096]{1,0:T(8,128)(2,1)S(1)}, bf16[64,4096]{1,0:T(8,128)(2,1)}, u32[]{:S(2)}) %copy-start.1) | copy-done | bytes 524312
  15.5 0.7 %copy-done.3 = s32[4]{0:T(128)S(1)} copy-done((s32[4]{0:T(128)S(1)}, s32[4]{0:T(128)}, u32[]{:S(2)}) %copy-start.3) | copy-done | bytes 40
  16.2 7.4 %project.3 = f32[8,64,128]{2,1,0:T(8,128)S(1)} custom-call(s32[4]{0:T(128)S(1)} %copy-done.3, bf16[1024,4096]{1,0:T(8,128)(2,1)} %acts.3, bf16[1024,14336]{1,0:T(8,128)(2,1)} %grads.3, bf16[64,4096]{1,0:T(8,128)(2,1)S(1)} %copy-done.1, bf16[64,14336]{1,0:T(8,128)(2,1)S(1)} %copy-done), custom_call_target="tpu_custom_call" | custom-call | flops 1207959552 | bytes 21233664 | tf_op jit(solution)/shard_map/project/pallas_call | solution.py:92
  23.6 0.1 collective-permute-start
  23.7 0.0 copy-done.5
  23.7 3.0 %collective-permute-start.6 = (f32[256,256]{1,0:T(8,128)S(1)}, f32[256,256]{1,0:T(8,128)S(1)}, u32[]{:S(2)}, u32[]{:S(2)}) collective-permute-start(f32[256,256]{1,0:T(8,128)S(1)} %collective-permute-done.5.refs_6_), channel_id=1, source_target_pairs={{0,2},{2,0},{4,6},{6,4},{8,10},{10,8},{12,14},{14,12},{16,18},{18,... | collective-permute-start | bytes 786440 | tf_op jit(solution)/shard_map/ppermute | solution.py:23
  26.7 0.0 collective-permute-done.9
  26.7 0.0 copy-done.4
  26.7 0.1 collective-permute-start.8
  26.8 0.0 collective-permute-done.10
  26.9 0.0 copy-start.6
  26.9 0.0 copy-start.16
  26.9 0.5 collective-permute-start.11
  27.4 4.1 %project.2 = f32[8,64,128]{2,1,0:T(8,128)S(1)} custom-call(s32[4]{0:T(128)S(1)} %copy-done.3, bf16[1024,4096]{1,0:T(8,128)(2,1)} %acts.3, bf16[1024,14336]{1,0:T(8,128)(2,1)} %grads.3, bf16[64,4096]{1,0:T(8,128)(2,1)S(1)} %copy-done.1, bf16[64,14336]{1,0:T(8,128)(2,1)S(1)} %copy-done), custom_call_target="tpu_custom_call" | custom-call | flops 1207959552 | bytes 21233664 | tf_op jit(solution)/shard_map/project/pallas_call | solution.py:92
  31.5 0.0 copy-done.6
  31.5 0.7 %copy-done.2 = f32[8,64,128]{2,1,0:T(8,128)} copy-done((f32[8,64,128]{2,1,0:T(8,128)}, f32[8,64,128]{2,1,0:T(8,128)S(1)}, u32[]{:S(2)}) %copy-start.2) | copy-done | bytes 262168
  32.3 0.0 collective-permute-done
  32.3 0.7 %copy-done.11 = f32[8,64,128]{2,1,0:T(8,128)} copy-done((f32[8,64,128]{2,1,0:T(8,128)}, f32[8,64,128]{2,1,0:T(8,128)S(1)}, u32[]{:S(2)}) %copy-start.11) | copy-done | bytes 262168
  33.0 2.3 %units.1 = f32[2,2,8,256]{3,2,1,0:T(8,128)} custom-call(f32[2,256,128]{2,1,0:T(8,128)} %bitcast.6, f32[2,256,128]{2,1,0:T(8,128)} %bitcast.7), custom_call_target="tpu_custom_call" | custom-call | tf_op jit(solution)/shard_map/units/pallas_call | solution.py:144
  35.2 0.7 %slice_bitcast_fusion = (f32[2,8,256]{2,1,0:T(8,128)S(1)}, f32[2,8,256]{2,1,0:T(8,128)S(1)}) fusion(f32[2,2,8,256]{3,2,1,0:T(8,128)} %units.1), kind=kLoop, calls=%fused_computation | loop fusion | bytes 65536 | tf_op jit(solution)/shard_map/squeeze | solution.py:234
  36.0 3.6 %collective-permute-start.1 = (f32[2,8,256]{2,1,0:T(8,128)S(1)}, f32[2,8,256]{2,1,0:T(8,128)S(1)}, u32[]{:S(2)}, u32[]{:S(2)}) collective-permute-start(f32[2,8,256]{2,1,0:T(8,128)S(1)} %get-tuple-element.6.refs_0_), channel_id=1, source_target_pairs={{0,1},{1,0},{2,3},{3,2},{4,5},{5,4},{6,7},{7,6},{8,9},{9,8},{10,11... | collective-permute-start | bytes 49160 | tf_op jit(solution)/shard_map/ppermute | solution.py:239
  39.6 0.0 collective-permute-done.4.refs_5_
  39.6 0.0 collective-permute-start.2
  39.6 1.7 %collective-permute-done.1.refs_1_ = f32[2,8,256]{2,1,0:T(8,128)S(1)} collective-permute-done((f32[2,8,256]{2,1,0:T(8,128)S(1)}, f32[2,8,256]{2,1,0:T(8,128)S(1)}, u32[]{:S(2)}, u32[]{:S(2)}) %collective-permute-start.1) | collective-permute-done | bytes 16416 | tf_op jit(solution)/shard_map/ppermute | solution.py:239
  41.3 0.7 %collective-permute-start.3 = (f32[2,8,256]{2,1,0:T(8,128)S(1)}, f32[2,8,256]{2,1,0:T(8,128)S(1)}, u32[]{:S(2)}, u32[]{:S(2)}) collective-permute-start(f32[2,8,256]{2,1,0:T(8,128)S(1)} %get-tuple-element.5), channel_id=1, source_target_pairs={{0,17},{1,16},{2,19},{3,18},{4,21},{5,20},{6,23},{7,22},{8,25},{9,... | collective-permute-start | bytes 49160 | tf_op jit(solution)/shard_map/ppermute | solution.py:239
  42.0 2.2 %collective-permute-done.2.refs_2_ = f32[2,8,256]{2,1,0:T(8,128)S(1)} collective-permute-done((f32[2,8,256]{2,1,0:T(8,128)S(1)}, f32[2,8,256]{2,1,0:T(8,128)S(1)}, u32[]{:S(2)}, u32[]{:S(2)}) %collective-permute-start.2) | collective-permute-done | bytes 16416 | tf_op jit(solution)/shard_map/ppermute | solution.py:23
  44.2 2.6 %collective-permute-done.3.refs_3_ = f32[2,8,256]{2,1,0:T(8,128)S(1)} collective-permute-done((f32[2,8,256]{2,1,0:T(8,128)S(1)}, f32[2,8,256]{2,1,0:T(8,128)S(1)}, u32[]{:S(2)}, u32[]{:S(2)}) %collective-permute-start.3) | collective-permute-done | bytes 16416 | tf_op jit(solution)/shard_map/ppermute | solution.py:239
  46.9 0.0 collective-permute-done.6.refs_7_
  46.9 0.0 collective-permute-done.8.refs_9_
  46.9 0.0 collective-permute-done.11.refs_11_
  46.9 0.5 copy-done.15
  47.5 0.1 copy-done.8
  47.6 0.1 copy-done.9
  47.7 0.7 %copy-done.10 = f32[256,256]{1,0:T(8,128)} copy-done((f32[256,256]{1,0:T(8,128)}, f32[256,256]{1,0:T(8,128)S(1)}, u32[]{:S(2)}) %copy-start.10) | copy-done | bytes 262168
  48.4 2.8 %scores.1 = f32[8,256]{1,0:T(8,128)} custom-call(f32[2,8,256]{2,1,0:T(8,128)} %copy-done.12, f32[2,8,256]{2,1,0:T(8,128)} %copy-done.13, f32[2,8,256]{2,1,0:T(8,128)} %copy-done.14, f32[2,8,256]{2,1,0:T(8,128)} %copy-done.15, f32[256,256]{1,0:T(8,128)} %refs_4_.1, f32[256,256]{1,0:T(8,128)} %copy-done.7, f32[256,256]{1,0:T(8,128)} %copy-done.5, ...), custom_call_target="tpu_custom_call" | custom-call | tf_op jit(solution)/shard_map/scores/pallas_call | solution.py:186
  51.2 0.7 %slice.41 = f32[4,256]{1,0:T(4,128)S(1)} slice(f32[8,256]{1,0:T(8,128)} %scores.1), slice={[4:8], [0:256]} | slice | bytes 8192 | tf_op jit(solution)/shard_map/slice | solution.py:244
  51.9 1.2 %collective-permute-start.12 = (f32[4,256]{1,0:T(4,128)S(1)}, f32[4,256]{1,0:T(4,128)S(1)}, u32[]{:S(2)}, u32[]{:S(2)}) collective-permute-start(f32[4,256]{1,0:T(4,128)S(1)} %slice.41), channel_id=1, source_target_pairs={{0,16},{2,18},{4,20},{6,22},{8,24},{10,26},{12,28},{14,30},{16,0},... | collective-permute-start | bytes 12296 | tf_op jit(solution)/shard_map/ppermute | solution.py:23
  53.1 3.3 %collective-permute-done.12 = f32[4,256]{1,0:T(4,128)S(1)} collective-permute-done((f32[4,256]{1,0:T(4,128)S(1)}, f32[4,256]{1,0:T(4,128)S(1)}, u32[]{:S(2)}, u32[]{:S(2)}) %collective-permute-start.12) | collective-permute-done | bytes 4128 | tf_op jit(solution)/shard_map/ppermute | solution.py:23
  56.4 0.7 %slice_add_fusion = f32[4,256]{1,0:T(4,128)S(1)} fusion(f32[4,256]{1,0:T(4,128)S(1)} %collective-permute-done.12, f32[8,256]{1,0:T(8,128)} %scores.1), kind=kLoop, calls=%fused_computation.4 | loop fusion | flops 1024 | bytes 12288 | tf_op jit(solution)/shard_map/add | solution.py:244
  57.1 0.7 %fusion = f32[4,256]{1,0:T(4,128)} fusion(f32[4,256]{1,0:T(4,128)S(1)} %slice_add_fusion, f32[2,256]{1,0:T(2,128)S(1)} %get-tuple-element.8, f32[2,256]{1,0:T(2,128)S(1)} %get-tuple-element.7, s32[256]{0:T(256)S(1)} %copy-done.16, pred[]{:T(512)S(6)} %eq.19, s32[4]{0:T(128)S(1)} %iota_add_fusion), kind=kLoop, calls=%fused_computation.6 | loop fusion | flops 4096 | bytes 13329 | tf_op jit(solution)/shard_map/jit(_where)/select_n | solution.py:253
  (26 shorter events, 0.1 us)
Async XLA Ops:
  0.0 9.5 %collective-permute-start.7 = (f32[256,256]{1,0:T(8,128)}, f32[256,256]{1,0:T(8,128)S(1)}, u32[]{:S(2)}, u32[]{:S(2)}) collective-permute-start(f32[256,256]{1,0:T(8,128)} %refs_4_.1), channel_id=1, source_target_pairs={{0,8},{2,10},{4,12},{6,14},{8,0},{10,2},{12,4},{14,6},{16,24},{18,... | collective-permute-start | bytes 786440 | tf_op jit(solution)/shard_map/ppermute | solution.py:23
  3.0 8.3 %collective-permute-start.5 = (f32[256,256]{1,0:T(8,128)}, f32[256,256]{1,0:T(8,128)S(1)}, u32[]{:S(2)}, u32[]{:S(2)}) collective-permute-start(f32[256,256]{1,0:T(8,128)} %refs_4_.1), channel_id=1, source_target_pairs={{0,4},{2,6},{4,0},{6,2},{8,12},{10,14},{12,8},{14,10},{16,20},{18,... | collective-permute-start | bytes 786440 | tf_op jit(solution)/shard_map/ppermute | solution.py:23
  9.5 17.2 %copy-start.4 = (f32[256,256]{1,0:T(8,128)}, f32[256,256]{1,0:T(8,128)S(1)}, u32[]{:S(2)}) copy-start(f32[256,256]{1,0:T(8,128)S(1)} %collective-permute-done.7.refs_8_) | copy-start | bytes 786436
  9.6 17.2 %collective-permute-start.9 = (f32[128,256]{1,0:T(8,128)S(1)}, f32[128,256]{1,0:T(8,128)S(1)}, u32[]{:S(2)}, u32[]{:S(2)}) collective-permute-start(f32[128,256]{1,0:T(8,128)S(1)} %slice.38), channel_id=1, source_target_pairs={{0,4},{2,6},{4,0},{6,2},{8,12},{10,14},{12,8},{14,10},{16,20},{18,... | collective-permute-start | bytes 393224 | tf_op jit(solution)/shard_map/ppermute | solution.py:23
  11.3 28.3 %collective-permute-start.4 = (f32[256,256]{1,0:T(8,128)}, f32[256,256]{1,0:T(8,128)S(1)}, u32[]{:S(2)}, u32[]{:S(2)}) collective-permute-start(f32[256,256]{1,0:T(8,128)} %refs_4_.1), channel_id=1, source_target_pairs={{0,2},{2,0},{4,6},{6,4},{8,10},{10,8},{12,14},{14,12},{16,18},{18,... | collective-permute-start | bytes 786440 | tf_op jit(solution)/shard_map/ppermute | solution.py:23
  11.3 12.4 %copy-start.5 = (f32[256,256]{1,0:T(8,128)}, f32[256,256]{1,0:T(8,128)S(1)}, u32[]{:S(2)}) copy-start(f32[256,256]{1,0:T(8,128)S(1)} %collective-permute-done.5.refs_6_) | copy-start | bytes 786436
  11.3 15.5 %collective-permute-start.10 = (f32[128,256]{1,0:T(8,128)S(1)}, f32[128,256]{1,0:T(8,128)S(1)}, u32[]{:S(2)}, u32[]{:S(2)}) collective-permute-start(f32[128,256]{1,0:T(8,128)S(1)} %slice.39), channel_id=1, source_target_pairs={{0,8},{2,10},{4,12},{6,14},{8,0},{10,2},{12,4},{14,6},{16,24},{18,... | collective-permute-start | bytes 393224 | tf_op jit(solution)/shard_map/ppermute | solution.py:23
  13.0 1.5 %copy-start = (bf16[64,14336]{1,0:T(8,128)(2,1)S(1)}, bf16[64,14336]{1,0:T(8,128)(2,1)}, u32[]{:S(2)}) copy-start(bf16[64,14336]{1,0:T(8,128)(2,1)} %proj_out.3) | copy-start | bytes 5505028
  14.5 1.0 %copy-start.1 = (bf16[64,4096]{1,0:T(8,128)(2,1)S(1)}, bf16[64,4096]{1,0:T(8,128)(2,1)}, u32[]{:S(2)}) copy-start(bf16[64,4096]{1,0:T(8,128)(2,1)} %proj_in.3) | copy-start | bytes 1572868
  15.5 0.7 %copy-start.3 = (s32[4]{0:T(128)S(1)}, s32[4]{0:T(128)}, u32[]{:S(2)}) copy-start(s32[4]{0:T(128)} %lengths.3) | copy-start | bytes 52
  23.6 8.7 %collective-permute-start = (f32[8,64,128]{2,1,0:T(8,128)S(1)}, f32[8,64,128]{2,1,0:T(8,128)S(1)}, u32[]{:S(2)}, u32[]{:S(2)}) collective-permute-start(f32[8,64,128]{2,1,0:T(8,128)S(1)} %project.3), channel_id=1, source_target_pairs={{0,1},{1,0},{2,3},{3,2},{4,5},{5,4},{6,7},{7,6},{8,9},{9,8},{10,11... | collective-permute-start | bytes 786440 | tf_op jit(solution)/shard_map/ppermute | solution.py:225
  23.7 23.2 %collective-permute-start.6 = (f32[256,256]{1,0:T(8,128)S(1)}, f32[256,256]{1,0:T(8,128)S(1)}, u32[]{:S(2)}, u32[]{:S(2)}) collective-permute-start(f32[256,256]{1,0:T(8,128)S(1)} %collective-permute-done.5.refs_6_), channel_id=1, source_target_pairs={{0,2},{2,0},{4,6},{6,4},{8,10},{10,8},{12,14},{14,12},{16,18},{18,... | collective-permute-start | bytes 786440 | tf_op jit(solution)/shard_map/ppermute | solution.py:23
  26.7 20.1 %collective-permute-start.8 = (f32[256,256]{1,0:T(8,128)S(1)}, f32[256,256]{1,0:T(8,128)S(1)}, u32[]{:S(2)}, u32[]{:S(2)}) collective-permute-start(f32[256,256]{1,0:T(8,128)S(1)} %collective-permute-done.7.refs_8_), channel_id=1, source_target_pairs={{0,2},{2,0},{4,6},{6,4},{8,10},{10,8},{12,14},{14,12},{16,18},{18,... | collective-permute-start | bytes 786440 | tf_op jit(solution)/shard_map/ppermute | solution.py:23
  26.9 4.7 %copy-start.6 = (f32[256,256]{1,0:T(8,128)}, f32[256,256]{1,0:T(8,128)S(1)}, u32[]{:S(2)}) copy-start(f32[256,256]{1,0:T(8,128)S(1)} %constant_dynamic-update-slice_fusion.refs_10_) | copy-start | bytes 786436
  26.9 30.3 %copy-start.16 = (s32[256]{0:T(256)S(1)}, s32[256]{0:T(256)}, u32[]{:S(2)}) copy-start(s32[256]{0:T(256)} %param.13) | copy-start | bytes 3076
  26.9 20.0 %collective-permute-start.11 = (f32[256,256]{1,0:T(8,128)S(1)}, f32[256,256]{1,0:T(8,128)S(1)}, u32[]{:S(2)}, u32[]{:S(2)}) collective-permute-start(f32[256,256]{1,0:T(8,128)S(1)} %constant_dynamic-update-slice_fusion.refs_10_), channel_id=1, source_target_pairs={{0,2},{2,0},{4,6},{6,4},{8,10},{10,8},{12,14},{14,12},{16,18},{18,... | collective-permute-start | bytes 786440 | tf_op jit(solution)/shard_map/ppermute | solution.py:23
  31.5 0.7 %copy-start.2 = (f32[8,64,128]{2,1,0:T(8,128)}, f32[8,64,128]{2,1,0:T(8,128)S(1)}, u32[]{:S(2)}) copy-start(f32[8,64,128]{2,1,0:T(8,128)S(1)} %project.2) | copy-start | bytes 786436
  32.3 0.7 %copy-start.11 = (f32[8,64,128]{2,1,0:T(8,128)}, f32[8,64,128]{2,1,0:T(8,128)S(1)}, u32[]{:S(2)}) copy-start(f32[8,64,128]{2,1,0:T(8,128)S(1)} %collective-permute-done) | copy-start | bytes 786436
  36.0 10.9 %copy-start.12 = (f32[2,8,256]{2,1,0:T(8,128)}, f32[2,8,256]{2,1,0:T(8,128)S(1)}, u32[]{:S(2)}) copy-start(f32[2,8,256]{2,1,0:T(8,128)S(1)} %get-tuple-element.6.refs_0_) | copy-start | bytes 49156
  36.0 5.4 %collective-permute-start.1 = (f32[2,8,256]{2,1,0:T(8,128)S(1)}, f32[2,8,256]{2,1,0:T(8,128)S(1)}, u32[]{:S(2)}, u32[]{:S(2)}) collective-permute-start(f32[2,8,256]{2,1,0:T(8,128)S(1)} %get-tuple-element.6.refs_0_), channel_id=1, source_target_pairs={{0,1},{1,0},{2,3},{3,2},{4,5},{5,4},{6,7},{7,6},{8,9},{9,8},{10,11... | collective-permute-start | bytes 49160 | tf_op jit(solution)/shard_map/ppermute | solution.py:239
  39.6 7.3 %copy-start.7 = (f32[256,256]{1,0:T(8,128)}, f32[256,256]{1,0:T(8,128)S(1)}, u32[]{:S(2)}) copy-start(f32[256,256]{1,0:T(8,128)S(1)} %collective-permute-done.4.refs_5_) | copy-start | bytes 786436
  39.6 4.6 %collective-permute-start.2 = (f32[2,8,256]{2,1,0:T(8,128)S(1)}, f32[2,8,256]{2,1,0:T(8,128)S(1)}, u32[]{:S(2)}, u32[]{:S(2)}) collective-permute-start(f32[2,8,256]{2,1,0:T(8,128)S(1)} %get-tuple-element.5), channel_id=1, source_target_pairs={{0,16},{2,18},{4,20},{6,22},{8,24},{10,26},{12,28},{14,30},{16,0},... | collective-permute-start | bytes 49160 | tf_op jit(solution)/shard_map/ppermute | solution.py:23
  41.3 5.6 %copy-start.13 = (f32[2,8,256]{2,1,0:T(8,128)}, f32[2,8,256]{2,1,0:T(8,128)S(1)}, u32[]{:S(2)}) copy-start(f32[2,8,256]{2,1,0:T(8,128)S(1)} %collective-permute-done.1.refs_1_) | copy-start | bytes 49156
  41.3 5.5 %collective-permute-start.3 = (f32[2,8,256]{2,1,0:T(8,128)S(1)}, f32[2,8,256]{2,1,0:T(8,128)S(1)}, u32[]{:S(2)}, u32[]{:S(2)}) collective-permute-start(f32[2,8,256]{2,1,0:T(8,128)S(1)} %get-tuple-element.5), channel_id=1, source_target_pairs={{0,17},{1,16},{2,19},{3,18},{4,21},{5,20},{6,23},{7,22},{8,25},{9,... | collective-permute-start | bytes 49160 | tf_op jit(solution)/shard_map/ppermute | solution.py:239
  44.2 2.7 %copy-start.14 = (f32[2,8,256]{2,1,0:T(8,128)}, f32[2,8,256]{2,1,0:T(8,128)S(1)}, u32[]{:S(2)}) copy-start(f32[2,8,256]{2,1,0:T(8,128)S(1)} %collective-permute-done.2.refs_2_) | copy-start | bytes 49156
  46.8 0.6 %copy-start.15 = (f32[2,8,256]{2,1,0:T(8,128)}, f32[2,8,256]{2,1,0:T(8,128)S(1)}, u32[]{:S(2)}) copy-start(f32[2,8,256]{2,1,0:T(8,128)S(1)} %collective-permute-done.3.refs_3_) | copy-start | bytes 49156
  46.9 0.7 %copy-start.8 = (f32[256,256]{1,0:T(8,128)}, f32[256,256]{1,0:T(8,128)S(1)}, u32[]{:S(2)}) copy-start(f32[256,256]{1,0:T(8,128)S(1)} %collective-permute-done.6.refs_7_) | copy-start | bytes 786436
  46.9 0.8 %copy-start.9 = (f32[256,256]{1,0:T(8,128)}, f32[256,256]{1,0:T(8,128)S(1)}, u32[]{:S(2)}) copy-start(f32[256,256]{1,0:T(8,128)S(1)} %collective-permute-done.8.refs_9_) | copy-start | bytes 786436
  47.7 0.7 %copy-start.10 = (f32[256,256]{1,0:T(8,128)}, f32[256,256]{1,0:T(8,128)S(1)}, u32[]{:S(2)}) copy-start(f32[256,256]{1,0:T(8,128)S(1)} %collective-permute-done.11.refs_11_) | copy-start | bytes 786436
  51.9 4.5 %collective-permute-start.12 = (f32[4,256]{1,0:T(4,128)S(1)}, f32[4,256]{1,0:T(4,128)S(1)}, u32[]{:S(2)}, u32[]{:S(2)}) collective-permute-start(f32[4,256]{1,0:T(4,128)S(1)} %slice.41), channel_id=1, source_target_pairs={{0,16},{2,18},{4,20},{6,22},{8,24},{10,26},{12,28},{14,30},{16,0},... | collective-permute-start | bytes 12296 | tf_op jit(solution)/shard_map/ppermute | solution.py:23
